TPU v7x, 32 devices: a whole 2x2x4 slice. The times are simulated.
32 devices in a mesh: dp: 8 (over y, x, core), win: 4 (over z).
Axes of the slice: x: 2, y: 2, z: 4, core: 2. Of those that a mesh axis runs over, the one named last changes fastest.
Arguments:
- features: bfloat16 [8, 2048, 512], P('dp', 'win')
- upstream_grad: bfloat16 [8, 2048, 256], P('dp', 'win'), may hold values from -48 to 48
- window_of: int32 [8, 2048], P('dp', 'win'), may hold values from 0 to 3, as said below
- window_slot: int32 [8, 2048], P('dp', 'win'), may hold values from 0 to 511
- gain: float32 [512], replicated, may hold values from 0.5 to 1.5
- bias: float32 [512], replicated, may hold values from -3 to 3
- w_qkv: bfloat16 [512, 768], replicated
Outputs:
- grad_in: bfloat16 [8, 2048, 512], P('dp', 'win')
- grad_qkv: float32 [512, 768], replicated
- grad_gain: float32 [512], replicated
- grad_bias: float32 [512], replicated
Inputs may be any that keep to these rules, and one draw needn't show every extreme that they name: `window_of`: in every scene each window receives exactly 512 points, whose window_slot values are distinct. The points of one tile (a block of 512 consecutive points) go to one window at most 256 times; every tile sends exactly 256 points to one window, and every window receives 256 points from one tile.
All inputs are finite; a program needn't handle non-finite values.
Results may differ from a plain program's by a relative error of at most 0.017.
Values may be sent and summed in bfloat16 or wider, within the bound.
A program may use at most 64 MiB of HBM per device.

v0:
```python
import jax
import jax.numpy as jnp
from jax import lax
from jax.sharding import PartitionSpec as P

HEADS = 4
HEAD = 64


epsilon = 1e-05


def normalize(window_rows, gain, bias, w_qkv):
    rows_f = window_rows.astype(jnp.float32)
    row_mean = jnp.mean(rows_f, axis=1, keepdims=True)
    centered = rows_f - row_mean
    row_var = jnp.mean(centered * centered, axis=1, keepdims=True)
    inv_std = lax.rsqrt(row_var + epsilon)
    unit_rows = centered * inv_std
    normed = (unit_rows * gain + bias).astype(jnp.bfloat16)
    qkv = jnp.dot(normed, w_qkv, preferred_element_type=jnp.float32).astype(jnp.bfloat16)
    return (unit_rows, inv_std, normed, qkv)


def attention_grads(qkv, window_upstream):
    inner = HEADS * HEAD
    score_scale = HEAD ** (-0.5)
    d_queries = []
    d_keys = []
    d_values = []
    for head_num in range(HEADS):
        col_start = head_num * HEAD
        queries = qkv[:, col_start : col_start + HEAD]
        key_block = qkv[:, inner + col_start : inner + col_start + HEAD]
        value_block = qkv[:, 2 * inner + col_start : 2 * inner + col_start + HEAD]
        outer = window_upstream[:, col_start : col_start + HEAD]
        scores = jnp.dot(queries, key_block.T, preferred_element_type=jnp.float32) * score_scale
        row_max = jnp.max(scores, axis=1, keepdims=True)
        exp_scores = jnp.exp(scores - row_max)
        attn_probs = exp_scores / jnp.sum(exp_scores, axis=1, keepdims=True)
        probs_bf = attn_probs.astype(jnp.bfloat16)
        grad_probs = jnp.dot(outer, value_block.T, preferred_element_type=jnp.float32)
        row_delta = jnp.sum(attn_probs * grad_probs, axis=1, keepdims=True)
        grad_scores = (attn_probs * (grad_probs - row_delta) * score_scale).astype(jnp.bfloat16)
        d_queries.append(
            jnp.dot(grad_scores, key_block, preferred_element_type=jnp.float32).astype(jnp.bfloat16)
        )
        d_keys.append(
            lax.dot_general(
                grad_scores, queries, (((0,), (0,)), ((), ())), preferred_element_type=jnp.float32
            ).astype(jnp.bfloat16)
        )
        d_values.append(
            lax.dot_general(
                probs_bf, outer, (((0,), (0,)), ((), ())), preferred_element_type=jnp.float32
            ).astype(jnp.bfloat16)
        )
    return jnp.concatenate(d_queries + d_keys + d_values, axis=1)


def finish(grad_rows, unit_rows, inv_std, normed, gain, w_qkv):
    grad_weight = lax.dot_general(
        normed, grad_rows, (((0,), (0,)), ((), ())), preferred_element_type=jnp.float32
    )
    grad_normed = lax.dot_general(
        grad_rows, w_qkv, (((1,), (1,)), ((), ())), preferred_element_type=jnp.float32
    )
    grad_gain = jnp.sum(grad_normed * unit_rows, axis=0)
    grad_bias = jnp.sum(grad_normed, axis=0)
    grad_hat = grad_normed * gain
    first_mean = jnp.mean(grad_hat, axis=1, keepdims=True)
    second_mean = jnp.mean(grad_hat * unit_rows, axis=1, keepdims=True)
    grad_window = (inv_std * (grad_hat - first_mean - unit_rows * second_mean)).astype(jnp.bfloat16)
    return (grad_window, grad_weight, grad_gain, grad_bias)


def per_device(features, upstream_grad, window_of, window_slot, gain, bias, w_qkv):
    win_count = lax.axis_size("win")
    point_count = features.shape[1]
    model_width = features.shape[2]
    inner = upstream_grad.shape[2]
    capacity = 2 * point_count // win_count
    tile_rows = features[0]
    tile_upstream = upstream_grad[0]
    target = window_of[0]
    slot_in = window_slot[0]
    member = (target[None, :] == jnp.arange(win_count, dtype=jnp.int32)[:, None]).astype(jnp.int32)
    send_rank = jnp.sum(member * (jnp.cumsum(member, axis=1) - 1), axis=0)
    position = target * capacity + send_rank
    send_rows = (
        jnp.zeros((win_count * capacity, model_width), jnp.bfloat16).at[position].set(tile_rows)
    )
    send_rows = send_rows.reshape(win_count, capacity, model_width)
    send_slots = jnp.full((win_count * capacity,), point_count, jnp.int32).at[position].set(slot_in)
    send_slots = send_slots.reshape(win_count, capacity)
    send_upstream = (
        jnp.zeros((win_count * capacity, inner), jnp.bfloat16).at[position].set(tile_upstream)
    )
    send_upstream = send_upstream.reshape(win_count, capacity, inner)
    got_rows, got_slots, got_upstream = (
        lax.all_to_all(send_rows, "win", split_axis=0, concat_axis=0, tiled=True),
        lax.all_to_all(send_slots, "win", split_axis=0, concat_axis=0, tiled=True),
        lax.all_to_all(send_upstream, "win", split_axis=0, concat_axis=0, tiled=True),
    )
    flat_slots = got_slots.reshape(-1)
    arrival = (
        jnp.zeros((point_count,), jnp.int32)
        .at[flat_slots]
        .set(jnp.arange(win_count * capacity, dtype=jnp.int32), mode="drop")
    )
    window_rows = got_rows.reshape(-1, model_width)[arrival]
    unit_rows, inv_std, normed, qkv = normalize(window_rows, gain, bias, w_qkv)
    window_upstream = got_upstream.reshape(-1, inner)[arrival]
    grad_rows = attention_grads(qkv, window_upstream)
    grad_window, grad_weight, grad_gain, grad_bias = finish(
        grad_rows, unit_rows, inv_std, normed, gain, w_qkv
    )
    live = (flat_slots < point_count)[:, None]
    safe_slots = jnp.minimum(flat_slots, point_count - 1)
    send_back = jnp.where(live, grad_window[safe_slots], jnp.zeros((), jnp.bfloat16))
    send_back = send_back.reshape(win_count, capacity, model_width)
    returned = lax.all_to_all(send_back, "win", split_axis=0, concat_axis=0, tiled=True)
    grad_in = returned.reshape(-1, model_width)[position]
    total_weight, total_gain, total_bias = lax.psum(
        (grad_weight, grad_gain, grad_bias), ("dp", "win")
    )
    window_count = lax.axis_size("dp") * win_count
    return (
        grad_in[None],
        total_weight / window_count,
        total_gain / window_count,
        total_bias / window_count,
    )


def solution(mesh):
    placed = (
        P("dp", "win", None),
        P("dp", "win", None),
        P("dp", "win"),
        P("dp", "win"),
        P(),
        P(),
        P(),
    )
    return jax.shard_map(
        per_device,
        mesh=mesh,
        in_specs=placed,
        out_specs=(P("dp", "win", None), P(), P(), P()),
        check_vma=False,
    )
```

profile of v0, /device:TPU:0, one launch (start us, length us, event | category | flops | bytes accessed | tf_op | source)
XLA Modules:
  0.0 250.0 jit_solution(13949534160117567843)
XLA Ops:
  7.2 0.8 fusion.76
  8.0 1.2 reduce-window.6
  9.6 0.8 select_reduce_fusion
  10.4 0.7 compare_select_fusion.2
  11.0 3.2 %scatter_custom_fusion = s32[1024]{0:T(1024)} fusion(s32[512]{0:T(512)S(1)} %bitcast.54, s32[512]{0:T(512)} %bitcast.62, s32[]{:T(128)} %constant.13.clone.1), kind=kCustom, calls=%fused_computation.133 | custom fusion | bytes 4608 | tf_op jit(solution)/shard_map/scatter | solution.py:94
  14.2 6.3 %all-to-all-start = ((s32[4,1,256]{2,1,0:T(1,128)}), s32[4,1,256]{2,1,0:T(1,128)S(1)}, u32[]{:S(2)}, u32[]{:S(2)}) async-start(s32[4,1,256]{2,1,0:T(1,128)} %bitcast.5), calls=%async_computation | async-start | bytes 8192 | tf_op jit(solution)/shard_map/all_to_all | solution.py:102
  20.5 3.5 %scatter_custom_fusion.3 = bf16[1024,256]{1,0:T(8,128)(2,1)} fusion(s32[512]{0:T(512)S(1)} %bitcast.55, bf16[1,512,256]{2,1,0:T(8,128)(2,1)} %param.8, bf16[]{:T(256)} %constant.18.clone.1), kind=kCustom, calls=%fused_computation.83 | custom fusion | bytes 786434 | tf_op jit(solution)/shard_map/scatter | solution.py:97
  24.1 2.0 all-to-all-done
  26.1 3.5 %all-to-all-start.2 = ((bf16[4,256,256]{2,1,0:T(8,128)(2,1)}), bf16[4,256,256]{2,1,0:T(8,128)(2,1)S(1)}, u32[]{:S(2)}, u32[]{:S(2)}) async-start(bf16[4,256,256]{2,1,0:T(8,128)(2,1)} %bitcast.12), calls=%async_computation.2 | async-start | bytes 1048576 | tf_op jit(solution)/shard_map/all_to_all | solution.py:103
  29.6 3.5 %scatter_custom_fusion.1 = bf16[1024,512]{1,0:T(8,128)(2,1)} fusion(s32[512]{0:T(512)S(1)} %bitcast.56, bf16[1,512,512]{2,1,0:T(8,128)(2,1)S(1)} %copy-done.1, bf16[]{:T(256)} %constant.18.clone.1), kind=kCustom, calls=%fused_computation.76 | custom fusion | bytes 1572866 | tf_op jit(solution)/shard_map/scatter | solution.py:91
  33.1 10.0 %all-to-all-done.2 = bf16[4,256,256]{2,1,0:T(8,128)(2,1)S(1)} async-done(((bf16[4,256,256]{2,1,0:T(8,128)(2,1)}), bf16[4,256,256]{2,1,0:T(8,128)(2,1)S(1)}, u32[]{:S(2)}, u32[]{:S(2)}) %all-to-all-start.2) | async-done | bytes 524320 | tf_op jit(solution)/shard_map/all_to_all | solution.py:103
  43.1 3.5 %all-to-all-start.1 = ((bf16[4,256,512]{2,1,0:T(8,128)(2,1)}), bf16[4,256,512]{2,1,0:T(8,128)(2,1)S(1)}, u32[]{:S(2)}, u32[]{:S(2)}) async-start(bf16[4,256,512]{2,1,0:T(8,128)(2,1)} %bitcast.7), calls=%async_computation.1 | async-start | bytes 2097152 | tf_op jit(solution)/shard_map/all_to_all | solution.py:101
  46.7 4.5 %scatter_custom_fusion.2 = s32[512]{0:T(512)S(1)} fusion(s32[1024]{0:T(1024)S(1)} %bitcast.61, s32[1024]{0:T(1024)S(1)} %iota.14, s32[]{:T(128)} %constant.15.clone.1), kind=kCustom, calls=%fused_computation.140 | custom fusion | bytes 2052 | tf_op jit(solution)/shard_map/scatter | solution.py:109
  51.2 2.0 gather_fusion.1
  53.2 18.6 %all-to-all-done.1 = bf16[4,256,512]{2,1,0:T(8,128)(2,1)S(1)} async-done(((bf16[4,256,512]{2,1,0:T(8,128)(2,1)}), bf16[4,256,512]{2,1,0:T(8,128)(2,1)S(1)}, u32[]{:S(2)}, u32[]{:S(2)}) %all-to-all-start.1) | async-done | bytes 1048608 | tf_op jit(solution)/shard_map/all_to_all | solution.py:101
  71.8 2.0 gather_fusion
  74.3 0.7 convolution_convert_fusion
  75.0 0.4 fusion.91
  75.7 0.4 fusion.89
  76.6 0.4 multiply_reduce_fusion
  77.7 0.4 multiply_reduce_fusion.2
  83.6 1.0 fusion.24
  84.6 0.4 fusion.23
  85.0 4.0 %gather_fusion.2 = bf16[1024,512]{1,0:T(8,128)(2,1)S(1)} fusion(bf16[512,512]{1,0:T(8,128)(2,1)S(1)} %fusion.23, s32[1024]{0:T(1024)S(1)} %broadcast_clamp_fusion), kind=kCustom, calls=%fused_computation.2 | custom fusion | bytes 2101248 | tf_op jit(solution)/shard_map/gather | solution.py:120
  89.0 1.2 broadcast_select_fusion
  90.2 3.6 %all-to-all-start.3 = ((bf16[4,256,512]{2,1,0:T(8,128)(2,1)}), bf16[4,256,512]{2,1,0:T(8,128)(2,1)S(1)}, u32[]{:S(2)}, u32[]{:S(2)}) async-start(bf16[4,256,512]{2,1,0:T(8,128)(2,1)} %broadcast_select_fusion), calls=%async_computation.3 | async-start | bytes 2097152 | tf_op jit(solution)/shard_map/all_to_all | solution.py:122
  93.9 2.0 fusion.81
  95.9 47.0 %all-reduce = (f32[512]{0:T(512)S(1)}, f32[512]{0:T(512)S(1)}) all-reduce(f32[512]{0:T(512)S(1)} %get-tuple-element.4, f32[512]{0:T(512)S(1)} %get-tuple-element.7), channel_id=1, replica_groups=mesh['dp'=8,'win'=4] {'dp','win'}, use_global_device_ids=true, to_apply=%region_25.26 | all-reduce | flops 1024 | bytes 8192 | tf_op jit(solution)/shard_map/psum | solution.py:124
  142.9 0.6 broadcast_multiply_fusion.1
  143.5 94.4 %all-reduce.3.cloned.1.call-done = f32[512,768]{1,0:T(8,128)} async-done(((f32[512,768]{1,0:T(8,128)}), f32[512,768]{1,0:T(8,128)}) %all-reduce.3.cloned.1.call-update) | async-done | bytes 1572880 | tf_op jit(solution)/shard_map/psum | solution.py:124
  237.9 2.7 %broadcast_multiply_fusion = f32[512,768]{1,0:T(8,128)} fusion(f32[512,768]{1,0:T(8,128)} %all-reduce.3.cloned.1.call-done), kind=kLoop, calls=%fused_computation.75 | loop fusion | flops 393216 | bytes 3145728 | tf_op jit(solution)/shard_map/div | solution.py:130
  240.6 2.6 %gather_fusion.3 = bf16[512,512]{1,0:T(8,128)(2,1)} fusion(bf16[1024,512]{1,0:T(8,128)(2,1)S(1)} %bitcast.45, s32[1024]{0:T(1024)S(1)} %pad_clamp_fusion), kind=kCustom, calls=%fused_computation.3 | custom fusion | bytes 1050624 | tf_op jit(solution)/shard_map/gather | solution.py:123
  (54 shorter events, 8.0 us)
Async XLA Ops:
  7.2 67.1 %copy-start = (bf16[512,768]{1,0:T(8,128)(2,1)S(1)}, bf16[512,768]{1,0:T(8,128)(2,1)}, u32[]{:S(2)}) copy-start(bf16[512,768]{1,0:T(8,128)(2,1)} %param.13) | copy-start | bytes 2359300
  7.2 22.4 %copy-start.1 = (bf16[1,512,512]{2,1,0:T(8,128)(2,1)S(1)}, bf16[1,512,512]{2,1,0:T(8,128)(2,1)}, u32[]{:S(2)}) copy-start(bf16[1,512,512]{2,1,0:T(8,128)(2,1)} %param.7) | copy-start | bytes 1572868
  14.2 11.9 %all-to-all-start = ((s32[4,1,256]{2,1,0:T(1,128)}), s32[4,1,256]{2,1,0:T(1,128)S(1)}, u32[]{:S(2)}, u32[]{:S(2)}) async-start(s32[4,1,256]{2,1,0:T(1,128)} %bitcast.5), calls=%async_computation | async-start | bytes 8192 | tf_op jit(solution)/shard_map/all_to_all | solution.py:102
  26.1 17.0 %all-to-all-start.2 = ((bf16[4,256,256]{2,1,0:T(8,128)(2,1)}), bf16[4,256,256]{2,1,0:T(8,128)(2,1)S(1)}, u32[]{:S(2)}, u32[]{:S(2)}) async-start(bf16[4,256,256]{2,1,0:T(8,128)(2,1)} %bitcast.12), calls=%async_computation.2 | async-start | bytes 1048576 | tf_op jit(solution)/shard_map/all_to_all | solution.py:103
  43.1 28.7 %all-to-all-start.1 = ((bf16[4,256,512]{2,1,0:T(8,128)(2,1)}), bf16[4,256,512]{2,1,0:T(8,128)(2,1)S(1)}, u32[]{:S(2)}, u32[]{:S(2)}) async-start(bf16[4,256,512]{2,1,0:T(8,128)(2,1)} %bitcast.7), calls=%async_computation.1 | async-start | bytes 2097152 | tf_op jit(solution)/shard_map/all_to_all | solution.py:101
  71.8 2.5 copy-start.4
  71.8 2.5 copy-start.5
  83.6 1.0 copy-start.2
  90.2 3.7 %copy-start.3 = (bf16[512,768]{0,1:T(8,128)(2,1)S(1)}, bf16[512,768]{0,1:T(8,128)(2,1)}, u32[]{:S(2)}) copy-start(bf16[512,768]{0,1:T(8,128)(2,1)} %copy-done.2) | copy-start | bytes 2359300
  90.2 150.4 %all-to-all-start.3 = ((bf16[4,256,512]{2,1,0:T(8,128)(2,1)}), bf16[4,256,512]{2,1,0:T(8,128)(2,1)S(1)}, u32[]{:S(2)}, u32[]{:S(2)}) async-start(bf16[4,256,512]{2,1,0:T(8,128)(2,1)} %broadcast_select_fusion), calls=%async_computation.3 | async-start | bytes 2097152 | tf_op jit(solution)/shard_map/all_to_all | solution.py:122
  93.8 144.1 %all-reduce.3.cloned.1.call-start = ((), (), s32[]{:S(2)}) async-start(), calls=%async_computation.4 | async-start | bytes 3145728 | tf_op jit(solution)/shard_map/psum | solution.py:124
Sparse Core Ops, SparseCore 0:
  100.5 137.3 all-reduce.2
where the time goes:
time: 251 us; the launch traced here: 250 us
  waiting for transfers between devices  125 us (50%)
  blocking collectives  47 us (19%)
  local copies, waits for them, and re-layouts  25.4 us (10%)
  starting transfers between devices  17 us (7%)
  between operations  14.4 us (6%)
  other arithmetic  10.9 us (4%)
  matrix products  10.3 us (4%)
    psum x1, waiting for transfers between devices, per_device(): lax.psum((grad_weight, grad_gain, grad_bias), ('dp', 'win'))  94.4 us
    psum x1, blocking collectives, per_device(): lax.psum((grad_weight, grad_gain, grad_bias), ('dp', 'win'))  47 us
    all_to_all x1, waiting for transfers between devices, per_device(): lax.all_to_all(send_rows, 'win', split_axis=0, concat_axis=0, tiled=True)  18.6 us
    all_to_all x1, waiting for transfers between devices, per_device(): lax.all_to_all(send_upstream, 'win', split_axis=0, concat_axis=0, tiled=T...  10 us
    all_to_all x1, starting transfers between devices, per_device(): lax.all_to_all(send_slots, 'win', split_axis=0, concat_axis=0, tiled=True)  6.32 us
  transfers between devices with their start and end apart: 5, of which 4 were waited for; matrix products, arithmetic and copies ran while one was open for 7% of the time, Pallas kernels for 0%

commit v1 on v0

--- a/solution.py
+++ b/solution.py
@@ -1,6 +1,8 @@
 import jax
 import jax.numpy as jnp
 from jax import lax
+from jax.experimental import pallas as pl
+from jax.experimental.pallas import tpu as pltpu
 from jax.sharding import PartitionSpec as P
 
 HEADS = 4
@@ -84,8 +86,9 @@
     tile_upstream = upstream_grad[0]
     target = window_of[0]
     slot_in = window_slot[0]
-    member = (target[None, :] == jnp.arange(win_count, dtype=jnp.int32)[:, None]).astype(jnp.int32)
-    send_rank = jnp.sum(member * (jnp.cumsum(member, axis=1) - 1), axis=0)
+    point = jnp.arange(point_count, dtype=jnp.int32)
+    earlier = (target[None, :] == target[:, None]) & (point[None, :] < point[:, None])
+    send_rank = jnp.sum(earlier.astype(jnp.int32), axis=1)
     position = target * capacity + send_rank
     send_rows = (
         jnp.zeros((win_count * capacity, model_width), jnp.bfloat16).at[position].set(tile_rows)
@@ -131,6 +134,368 @@
         total_gain / window_count,
         total_bias / window_count,
     )
+
+
+BF = jnp.bfloat16
+F32 = jnp.float32
+PAIR = 2 * HEAD
+NT = (((1,), (1,)), ((), ()))
+TN = (((0,), (0,)), ((), ()))
+
+POS, QK, VU, DQK, DV, RZ, GZ, SZ = (4 * i for i in range(8))
+R0, R1, R2, G0, G1, G2, S0, S1, S2 = range(32, 41)
+N_SEM = 41
+
+
+def fused(
+    feat,
+    up,
+    pos,
+    gain,
+    bias,
+    w,
+    grad_in,
+    gw_out,
+    gs_out,
+    unit,
+    normed,
+    inv,
+    pos_all,
+    send_qk,
+    send_vu,
+    got_qk,
+    got_vu,
+    hot,
+    hot_t,
+    win_qk,
+    probs,
+    d_win,
+    send_dqk,
+    send_dv,
+    got_dqk,
+    got_dv,
+    rows,
+    acc,
+    stage,
+    rb0,
+    rb1,
+    rb2,
+    rbz,
+    total,
+    small_send,
+    small_got,
+    small_z,
+    ssem,
+    rsem,
+):
+    n = feat.shape[0]
+    half = n // 2
+    inner = HEADS * HEAD
+    scale = HEAD ** (-0.5)
+    dp = lax.axis_index("dp")
+    me = lax.axis_index("win")
+    c = dp % 2
+    bx = (dp // 2) % 2
+    by = dp // 4
+    peer_c = dp + 1 - 2 * c
+    peer_x = dp + 2 - 4 * bx
+    peer_y = dp + 4 - 8 * by
+    peers = [(me + d) % HEADS for d in (2, 1, 3)]
+
+    def remote(source, target, s, r, where):
+        return pltpu.make_async_remote_copy(
+            src_ref=source,
+            dst_ref=target,
+            send_sem=ssem.at[s],
+            recv_sem=rsem.at[r],
+            device_id=where,
+            device_id_type=pl.DeviceIdType.MESH,
+        )
+
+    places = [(dp, t) for t in peers] + [(p, me) for p in (peer_c, peer_x, peer_y)]
+    barrier = pltpu.get_barrier_semaphore()
+    for place in places:
+        pl.semaphore_signal(barrier, inc=1, device_id=place, device_id_type=pl.DeviceIdType.MESH)
+    pl.semaphore_wait(barrier, len(places))
+
+    def block(ref, t, size):
+        return ref.at[pl.ds(pl.multiple_of(t * size, size), size)]
+
+    def exchange(source, target, base, size):
+        for t in peers:
+            remote(block(source, t, size), block(target, me, size), base + t, base + me, (dp, t)).start()
+
+    def arrived(target, base, size):
+        for t in peers:
+            remote(block(target, t, size), block(target, t, size), base + t, base + t, (dp, t)).wait_recv()
+
+    for t in peers:
+        remote(pos, pos_all.at[me], POS + t, POS + me, (dp, t)).start()
+    pos_all[me] = pos[...]
+
+    x = feat[...].astype(F32)
+    centered = x - jnp.mean(x, axis=1, keepdims=True)
+    inv_std = lax.rsqrt(jnp.mean(centered * centered, axis=1, keepdims=True) + epsilon)
+    u = centered * inv_std
+    unit[...] = u
+    inv[...] = inv_std
+    normed[...] = (u * gain[...] + bias[...]).astype(BF)
+    qk = jnp.dot(normed[...], w[:, : 2 * inner], preferred_element_type=F32).astype(BF)
+    for h in range(HEADS):
+        send_qk[h * n : (h + 1) * n, :HEAD] = qk[:, h * HEAD : (h + 1) * HEAD]
+        send_qk[h * n : (h + 1) * n, HEAD:] = qk[:, inner + h * HEAD : inner + (h + 1) * HEAD]
+    exchange(send_qk, got_qk, QK, n)
+    v = jnp.dot(normed[...], w[:, 2 * inner :], preferred_element_type=F32).astype(BF)
+    for h in range(HEADS):
+        send_vu[h * n : (h + 1) * n, :HEAD] = v[:, h * HEAD : (h + 1) * HEAD]
+        send_vu[h * n : (h + 1) * n, HEAD:] = up[:, h * HEAD : (h + 1) * HEAD]
+    exchange(send_vu, got_vu, VU, n)
+    mine = pl.ds(pl.multiple_of(me * n, n), n)
+    got_qk[mine, :] = send_qk[mine, :]
+    got_vu[mine, :] = send_vu[mine, :]
+
+    for t in peers:
+        remote(pos_all.at[t], pos_all.at[t], POS + t, POS + t, (dp, t)).wait_recv()
+    for t in range(HEADS):
+        row = jnp.broadcast_to(pos_all[t, 0:1, :], (128, n))
+        column = row.astype(F32).T.astype(jnp.int32)
+        row = jnp.broadcast_to(pos_all[t, 0:1, :], (n, n))
+        slots = lax.broadcasted_iota(jnp.int32, (n, n), 0)
+        lanes = lax.broadcasted_iota(jnp.int32, (n, 128), 1)
+
+        @pl.loop(0, HEADS)
+        def _(k):
+            hot[pl.ds(pl.multiple_of(k * n, n), n), t * n : (t + 1) * n] = jnp.where(
+                slots + k * n == row, 1.0, 0.0
+            ).astype(BF)
+
+        for j in range(HEADS * n // 128):
+            hot_t[t * n : (t + 1) * n, j * 128 : (j + 1) * 128] = jnp.where(
+                lanes + j * 128 == column, 1.0, 0.0
+            ).astype(BF)
+
+    arrived(got_qk, QK, n)
+
+    @pl.loop(0, HEADS)
+    def _(k):
+        here = pl.ds(pl.multiple_of(k * n, n), n)
+        both = jnp.dot(hot[here, :], got_qk[...], preferred_element_type=F32).astype(BF)
+        win_qk[here, :] = both
+        s = lax.dot_general(both[:, HEAD:], both[:, :HEAD], NT, preferred_element_type=F32) * scale
+        e = jnp.exp(s - jnp.max(s, axis=0, keepdims=True))
+        probs[here, :] = e * (1.0 / jnp.sum(e, axis=0, keepdims=True))
+
+    arrived(got_vu, VU, n)
+
+    @pl.loop(0, HEADS)
+    def _(k):
+        here = pl.ds(pl.multiple_of(k * n, n), n)
+        both = jnp.dot(hot[here, :], got_vu[...], preferred_element_type=F32).astype(BF)
+        values, outer = both[:, :HEAD], both[:, HEAD:]
+        p = probs[here, :]
+        d_values = jnp.dot(p.astype(BF), outer, preferred_element_type=F32).astype(BF)
+        gp = lax.dot_general(values, outer, NT, preferred_element_type=F32)
+        delta = jnp.sum(p * gp, axis=0, keepdims=True)
+        gs = (p * (gp - delta) * scale).astype(BF)
+        queries, keys = win_qk[here, :HEAD], win_qk[here, HEAD:]
+        d_win[here, :HEAD] = lax.dot_general(gs, keys, TN, preferred_element_type=F32).astype(BF)
+        d_win[here, HEAD:PAIR] = jnp.dot(gs, queries, preferred_element_type=F32).astype(BF)
+        d_win[here, PAIR : PAIR + HEAD] = d_values
+        d_win[here, PAIR + HEAD :] = jnp.zeros((n, HEAD), BF)
+
+    def to_tile(t, dqk_ref, dv_ref, slot):
+        here = pl.ds(pl.multiple_of(t * n, n), n)
+        back = jnp.dot(hot_t[here, :], d_win[...], preferred_element_type=F32).astype(BF)
+        dqk_ref[pl.ds(pl.multiple_of(slot * n, n), n), :] = back[:, :PAIR]
+        place = pl.ds(pl.multiple_of(slot * half, half), half)
+        dv_ref[place, :HEAD] = back[:half, PAIR : PAIR + HEAD]
+        dv_ref[place, HEAD:] = back[half:, PAIR : PAIR + HEAD]
+
+    for t in peers:
+        to_tile(t, send_dqk, send_dv, t)
+        remote(block(send_dqk, t, n), block(got_dqk, me, n), DQK + t, DQK + me, (dp, t)).start()
+        remote(block(send_dv, t, half), block(got_dv, me, half), DV + t, DV + me, (dp, t)).start()
+    to_tile(me, got_dqk, got_dv, me)
+    arrived(got_dqk, DQK, n)
+    arrived(got_dv, DV, half)
+    for h in range(HEADS):
+        rows[:, h * HEAD : (h + 1) * HEAD] = got_dqk[h * n : (h + 1) * n, :HEAD]
+        rows[:, inner + h * HEAD : inner + (h + 1) * HEAD] = got_dqk[h * n : (h + 1) * n, HEAD:]
+        v_at = 2 * inner + h * HEAD
+        rows[:half, v_at : v_at + HEAD] = got_dv[h * half : (h + 1) * half, :HEAD]
+        rows[half:, v_at : v_at + HEAD] = got_dv[h * half : (h + 1) * half, HEAD:]
+
+    g = lax.dot_general(normed[...], rows[...], TN, preferred_element_type=F32)
+    acc[...] = g
+    stage[...] = g.astype(BF)
+    depth = acc.shape[0]
+    d1, d2, d3, d4 = depth // 2, depth // 4, depth // 8, depth // 32
+    b1 = (1 - c) * bx + c * by
+    b2 = (1 - c) * by + c * bx
+    peer_1 = (1 - c) * peer_x + c * peer_y
+    peer_2 = (1 - c) * peer_y + c * peer_x
+    off0 = c * d1
+    off1 = off0 + b1 * d2
+    off2 = off1 + b2 * d3
+    off3 = off2 + me * d4
+
+    def at(off, size):
+        return pl.ds(pl.multiple_of(off, size), size)
+
+    other0 = at((1 - c) * d1, d1)
+    other1 = at(off0 + (1 - b1) * d2, d2)
+    other2 = at(off1 + (1 - b2) * d3, d3)
+
+    step0 = remote(stage.at[other0], rb0, R0, R0, (peer_c, me))
+    step0.start()
+
+    gn = lax.dot_general(rows[...], w[...], NT, preferred_element_type=F32)
+    u = unit[...]
+    row_id = lax.broadcasted_iota(jnp.int32, (8, gn.shape[1]), 0)
+    small = jnp.where(
+        row_id == 0,
+        jnp.sum(gn * u, axis=0, keepdims=True),
+        jnp.where(row_id == 1, jnp.sum(gn, axis=0, keepdims=True), 0.0),
+    )
+    small_send[0] = small
+    small0 = remote(small_send.at[0], small_got.at[0], S0, S0, (peer_c, me))
+    small0.start()
+    gh = gn * gain[...]
+    first = jnp.mean(gh, axis=1, keepdims=True)
+    second = jnp.mean(gh * u, axis=1, keepdims=True)
+    grad_in[...] = (inv[...] * (gh - first - u * second)).astype(BF)
+
+    step0.wait()
+    keep = at(off0, d1)
+    acc[keep, :] += rb0[...].astype(F32)
+    stage[keep, :] = acc[keep, :].astype(BF)
+    step1 = remote(stage.at[other1], rb1, R1, R1, (peer_1, me))
+    step1.start()
+    small0.wait()
+    small_send[1] = small_send[0] + small_got[0]
+    small1 = remote(small_send.at[1], small_got.at[1], S1, S1, (peer_x, me))
+    small1.start()
+
+    step1.wait()
+    keep = at(off1, d2)
+    acc[keep, :] += rb1[...].astype(F32)
+    stage[keep, :] = acc[keep, :].astype(BF)
+    step2 = remote(stage.at[other2], rb2, R2, R2, (peer_2, me))
+    step2.start()
+    small1.wait()
+    small_send[2] = small_send[1] + small_got[1]
+    small2 = remote(small_send.at[2], small_got.at[2], S2, S2, (peer_y, me))
+    small2.start()
+
+    step2.wait()
+    keep = at(off2, d3)
+    acc[keep, :] += rb2[...].astype(F32)
+    stage[keep, :] = acc[keep, :].astype(BF)
+    for t in peers:
+        remote(stage.at[at(off2 + t * d4, d4)], rbz.at[me], RZ + t, RZ + me, (dp, t)).start()
+    small2.wait()
+    small_send[3] = small_send[2] + small_got[2]
+    for t in peers:
+        remote(small_send.at[3], small_z.at[me], SZ + t, SZ + me, (dp, t)).start()
+    small_z[me] = small_send[3]
+
+    mine = at(off3, d4)
+    for t in peers:
+        remote(rbz.at[t], rbz.at[t], RZ + t, RZ + t, (dp, t)).wait_recv()
+    own = acc[mine, :]
+    for t in peers:
+        own += rbz[t].astype(F32)
+    windows = lax.axis_size("dp") * lax.axis_size("win")
+    total[mine, :] = (own * (1.0 / windows)).astype(BF)
+
+    for t in peers:
+        remote(total.at[mine], total.at[mine], GZ + t, GZ + me, (dp, t)).start()
+    for t in peers:
+        there = total.at[at(off2 + t * d4, d4)]
+        remote(there, there, GZ + t, GZ + t, (dp, t)).wait_recv()
+    back2 = remote(total.at[at(off2, d3)], total.at[at(off2, d3)], G2, G2, (peer_2, me))
+    back2.start()
+    for t in peers:
+        remote(small_z.at[t], small_z.at[t], SZ + t, SZ + t, (dp, t)).wait_recv()
+    gs_out[...] = (small_z[0] + small_z[1] + small_z[2] + small_z[3]) * (1.0 / windows)
+
+    back2.wait_send()
+    remote(total.at[other2], total.at[other2], G2, G2, (peer_2, me)).wait_recv()
+    back1 = remote(total.at[at(off1, d2)], total.at[at(off1, d2)], G1, G1, (peer_1, me))
+    back1.start()
+    back1.wait_send()
+    remote(total.at[other1], total.at[other1], G1, G1, (peer_1, me)).wait_recv()
+    back0 = remote(total.at[at(off0, d1)], total.at[at(off0, d1)], G0, G0, (peer_c, me))
+    back0.start()
+    gw_out[at(off0, d1), :] = total[at(off0, d1), :].astype(F32)
+    back0.wait_send()
+    remote(total.at[other0], total.at[other0], G0, G0, (peer_c, me)).wait_recv()
+    gw_out[other0, :] = total[other0, :].astype(F32)
+
+    for t in peers:
+        remote(pos, pos, POS + t, POS + t, (dp, t)).wait_send()
+        remote(block(send_qk, t, n), block(send_qk, t, n), QK + t, QK + t, (dp, t)).wait_send()
+        remote(block(send_vu, t, n), block(send_vu, t, n), VU + t, VU + t, (dp, t)).wait_send()
+        remote(block(send_dqk, t, n), block(send_dqk, t, n), DQK + t, DQK + t, (dp, t)).wait_send()
+        remote(block(send_dv, t, half), block(send_dv, t, half), DV + t, DV + t, (dp, t)).wait_send()
+        piece = stage.at[at(off2 + t * d4, d4)]
+        remote(piece, piece, RZ + t, RZ + t, (dp, t)).wait_send()
+        remote(total.at[mine], total.at[mine], GZ + t, GZ + t, (dp, t)).wait_send()
+        remote(small_send.at[3], small_send.at[3], SZ + t, SZ + t, (dp, t)).wait_send()
+
+
+def by_heads(features, upstream_grad, window_of, window_slot, gain, bias, w_qkv):
+    n, width = features.shape[1:]
+    cols = w_qkv.shape[1]
+    all_rows = HEADS * n
+    pos = jnp.broadcast_to(window_of * n + window_slot, (8, n))
+    vmem = pl.BlockSpec(memory_space=pltpu.VMEM)
+    grad_in, grad_w, small = pl.pallas_call(
+        fused,
+        out_shape=(
+            jax.ShapeDtypeStruct((n, width), BF),
+            jax.ShapeDtypeStruct((width, cols), F32),
+            jax.ShapeDtypeStruct((8, width), F32),
+        ),
+        in_specs=[vmem] * 6,
+        out_specs=(vmem, vmem, vmem),
+        scratch_shapes=[
+            pltpu.VMEM((n, width), F32),
+            pltpu.VMEM((n, width), BF),
+            pltpu.VMEM((n, 1), F32),
+            pltpu.VMEM((HEADS, 8, n), jnp.int32),
+            pltpu.VMEM((all_rows, PAIR), BF),
+            pltpu.VMEM((all_rows, PAIR), BF),
+            pltpu.VMEM((all_rows, PAIR), BF),
+            pltpu.VMEM((all_rows, PAIR), BF),
+            pltpu.VMEM((all_rows, all_rows), BF),
+            pltpu.VMEM((all_rows, all_rows), BF),
+            pltpu.VMEM((all_rows, PAIR), BF),
+            pltpu.VMEM((all_rows, n), F32),
+            pltpu.VMEM((all_rows, 2 * PAIR), BF),
+            pltpu.VMEM((all_rows, PAIR), BF),
+            pltpu.VMEM((all_rows // 2, PAIR), BF),
+            pltpu.VMEM((all_rows, PAIR), BF),
+            pltpu.VMEM((all_rows // 2, PAIR), BF),
+            pltpu.VMEM((n, cols), BF),
+            pltpu.VMEM((width, cols), F32),
+            pltpu.VMEM((width, cols), BF),
+            pltpu.VMEM((width // 2, cols), BF),
+            pltpu.VMEM((width // 4, cols), BF),
+            pltpu.VMEM((width // 8, cols), BF),
+            pltpu.VMEM((HEADS, width // 32, cols), BF),
+            pltpu.VMEM((width, cols), BF),
+            pltpu.VMEM((4, 8, width), F32),
+            pltpu.VMEM((3, 8, width), F32),
+            pltpu.VMEM((HEADS, 8, width), F32),
+            pltpu.SemaphoreType.DMA((N_SEM,)),
+            pltpu.SemaphoreType.DMA((N_SEM,)),
+        ],
+        compiler_params=pltpu.CompilerParams(
+            collective_id=0, has_side_effects=True, vmem_limit_bytes=56 * 2**20
+        ),
+    )(features[0], upstream_grad[0], pos, gain[None], bias[None], w_qkv)
+    return grad_in[None], grad_w, small[0], small[1]
 
 
 def solution(mesh):
@@ -143,8 +508,9 @@
         P(),
         P(),
     )
+    heads_fit = mesh.shape["win"] == HEADS and mesh.shape["dp"] == 8
     return jax.shard_map(
-        per_device,
+        by_heads if heads_fit else per_device,
         mesh=mesh,
         in_specs=placed,
         out_specs=(P("dp", "win", None), P(), P(), P()),

time: 251 us -> 100 us (0.40)
  waiting for transfers between devices: 125 us -> 0 us
  Pallas kernels: 0 us -> 92.2 us
  blocking collectives: 47 us -> 0 us
  local copies, waits for them, and re-layouts: 25.4 us -> 6.51 us
  starting transfers between devices: 17 us -> 0 us
  between operations: 14.4 us -> 0.64 us
  matrix products: 10.3 us -> 0 us
  other arithmetic: 10.9 us -> 0.7 us
    psum x1 -> x0, waiting for transfers between devices: 94.4 us -> none  [per_device(): lax.psum((grad_weight, grad_gain, grad_bias), ('dp', 'win'))]
    pallas_call x0 -> x1, Pallas kernels: none -> 92.2 us  [by_heads(): pl.pallas_call(fused, out_shape=(jax.ShapeDtypeStruct((n, width), BF), ja...]
    psum x1 -> x0, blocking collectives: 47 us -> none  [per_device(): lax.psum((grad_weight, grad_gain, grad_bias), ('dp', 'win'))]
    all_to_all x4 -> x0, waiting for transfers between devices: 30.7 us -> none  [the longest x1 18.6 us: per_device(): lax.all_to_all(send_rows, 'win', split_axis=0, concat_axis=0, tiled=True)]
    all_to_all x4 -> x0, starting transfers between devices: 17 us -> none  [the longest x1 6.32 us: per_device(): lax.all_to_all(send_slots, 'win', split_axis=0, concat_axis=0, tiled=True)]
    scatter x4 -> x0, local copies, waits for them, and re-layouts: 14.6 us -> none  [the longest x1 4.48 us: per_device(): arrival = jnp.zeros((point_count,), jnp.int32).at[flat_slots].set(jnp.ara...]
    gather x4 -> x0, local copies, waits for them, and re-layouts: 10.5 us -> none  [the longest x1 3.97 us: per_device(): grad_window[safe_slots]]
    dot_general x23 -> x0, matrix products: 10.3 us -> none  [the longest x1 2 us: finish(): lax.dot_general(normed, grad_rows, (((0,), (0,)), ((), ())), preferred_el...]
  transfers between devices with their start and end apart: 5 -> 0, of which waited for: 4 -> 0; matrix products, arithmetic and copies ran while one was open for 7% -> 0% of each run, Pallas kernels for 0% -> 0%
where the time goes in v1:
time: 100 us
  Pallas kernels  92.2 us (92%)
  local copies, waits for them, and re-layouts  6.51 us (7%)
    pallas_call x1, Pallas kernels, by_heads(): pl.pallas_call(fused, out_shape=(jax.ShapeDtypeStruct((n, width), BF), ja...  92.2 us
    unnamed x2, local copies, waits for them, and re-layouts  4.52 us

profile of v1, /device:TPU:0, one launch (start us, length us, event | category | flops | bytes accessed | tf_op | source)
XLA Modules:
  0.0 100.1 jit_solution(4051901716292691883)
XLA Ops:
  0.6 0.7 multiply_add_fusion
  1.3 0.6 broadcast_in_dim.17.pos
  1.9 92.2 %shard_map.102 = (bf16[512,512]{1,0:T(8,128)(2,1)}, f32[512,768]{1,0:T(8,128)}, f32[8,512]{1,0:T(8,128)}) custom-call(bf16[512,512]{1,0:T(8,128)(2,1)} %bitcast.8, bf16[512,256]{1,0:T(8,128)(2,1)} %bitcast.10, s32[8,512]{1,0:T(8,128)} %broadcast_in_dim.17.pos, f32[1,512]{1,0:T(1,128)} %bitcast.12, f32[1,512]{1,0:T(1,128)} %bitcast.13, bf16[512,768]{1,0:T(8,128)(2,1)} %w.1), custom_call_target="tpu_custom_call" | custom-call | tf_op jit(solution)/shard_map/pallas_call | solution.py:453
  94.2 1.4 %fusion = (f32[1,512]{1,0:T(1,128)}, f32[1,512]{1,0:T(1,128)}) fusion(f32[8,512]{1,0:T(8,128)} %get-tuple-element.9), kind=kLoop, calls=%fused_computation.1 | loop fusion | bytes 8192 | tf_op jit(solution)/shard_map/slice | solution.py:498
  95.6 1.9 %copy.13 = bf16[1,512,512]{2,1,0:T(8,128)(2,1)} copy(bf16[1,512,512]{2,1,0:T(8,128)(2,1)} %bitcast.9) | data formatting | bytes 1048576
  97.4 2.7 %copy.14 = f32[512,768]{1,0:T(8,128)} copy(f32[512,768]{1,0:T(8,128)} %get-tuple-element.17) | data formatting | bytes 3145728

commit v2 on v1

--- a/solution.py
+++ b/solution.py
@@ -142,9 +142,9 @@
 NT = (((1,), (1,)), ((), ()))
 TN = (((0,), (0,)), ((), ()))
 
-POS, QK, VU, DQK, DV, RZ, GZ, SZ = (4 * i for i in range(8))
-R0, R1, R2, G0, G1, G2, S0, S1, S2 = range(32, 41)
-N_SEM = 41
+POS, QK, U, V, DQK, DV, RZ, GZ, SZ = (4 * i for i in range(9))
+R0, R1, R2, G0, G1, G2, S0, S1, S2 = range(36, 45)
+N_SEM = 45
 
 
 def fused(
@@ -162,13 +162,18 @@
     inv,
     pos_all,
     send_qk,
-    send_vu,
+    send_u,
+    send_v,
     got_qk,
-    got_vu,
+    got_u,
+    got_v,
+    tile_qku,
+    tile_v,
     hot,
     hot_t,
-    win_qk,
+    win_qku,
     probs,
+    d_val,
     d_win,
     send_dqk,
     send_dv,
@@ -233,6 +238,11 @@
         remote(pos, pos_all.at[me], POS + t, POS + me, (dp, t)).start()
     pos_all[me] = pos[...]
 
+    for h in range(HEADS):
+        send_u[h * half : (h + 1) * half, :HEAD] = up[:half, h * HEAD : (h + 1) * HEAD]
+        send_u[h * half : (h + 1) * half, HEAD:] = up[half:, h * HEAD : (h + 1) * HEAD]
+    exchange(send_u, got_u, U, half)
+
     x = feat[...].astype(F32)
     centered = x - jnp.mean(x, axis=1, keepdims=True)
     inv_std = lax.rsqrt(jnp.mean(centered * centered, axis=1, keepdims=True) + epsilon)
@@ -247,12 +257,14 @@
     exchange(send_qk, got_qk, QK, n)
     v = jnp.dot(normed[...], w[:, 2 * inner :], preferred_element_type=F32).astype(BF)
     for h in range(HEADS):
-        send_vu[h * n : (h + 1) * n, :HEAD] = v[:, h * HEAD : (h + 1) * HEAD]
-        send_vu[h * n : (h + 1) * n, HEAD:] = up[:, h * HEAD : (h + 1) * HEAD]
-    exchange(send_vu, got_vu, VU, n)
+        send_v[h * half : (h + 1) * half, :HEAD] = v[:half, h * HEAD : (h + 1) * HEAD]
+        send_v[h * half : (h + 1) * half, HEAD:] = v[half:, h * HEAD : (h + 1) * HEAD]
+    exchange(send_v, got_v, V, half)
     mine = pl.ds(pl.multiple_of(me * n, n), n)
     got_qk[mine, :] = send_qk[mine, :]
-    got_vu[mine, :] = send_vu[mine, :]
+    mine = pl.ds(pl.multiple_of(me * half, half), half)
+    got_u[mine, :] = send_u[mine, :]
+    got_v[mine, :] = send_v[mine, :]
 
     for t in peers:
         remote(pos_all.at[t], pos_all.at[t], POS + t, POS + t, (dp, t)).wait_recv()
@@ -274,50 +286,74 @@
                 lanes + j * 128 == column, 1.0, 0.0
             ).astype(BF)
 
+    arrived(got_u, U, half)
+    for t in range(HEADS):
+        packed = got_u[t * half : (t + 1) * half, :]
+        tile_qku[t * n : t * n + half, PAIR : PAIR + HEAD] = packed[:, :HEAD]
+        tile_qku[t * n + half : (t + 1) * n, PAIR : PAIR + HEAD] = packed[:, HEAD:]
+    tile_qku[:, PAIR + HEAD :] = jnp.zeros((HEADS * n, HEAD), BF)
     arrived(got_qk, QK, n)
+    tile_qku[:, :PAIR] = got_qk[...]
 
     @pl.loop(0, HEADS)
     def _(k):
         here = pl.ds(pl.multiple_of(k * n, n), n)
-        both = jnp.dot(hot[here, :], got_qk[...], preferred_element_type=F32).astype(BF)
-        win_qk[here, :] = both
-        s = lax.dot_general(both[:, HEAD:], both[:, :HEAD], NT, preferred_element_type=F32) * scale
+        three = jnp.dot(hot[here, :], tile_qku[...], preferred_element_type=F32).astype(BF)
+        win_qku[here, :] = three
+        queries, keys = three[:, :HEAD], three[:, HEAD:PAIR]
+        s = lax.dot_general(keys, queries, NT, preferred_element_type=F32) * scale
         e = jnp.exp(s - jnp.max(s, axis=0, keepdims=True))
-        probs[here, :] = e * (1.0 / jnp.sum(e, axis=0, keepdims=True))
-
-    arrived(got_vu, VU, n)
+        p = e * (1.0 / jnp.sum(e, axis=0, keepdims=True))
+        probs[here, :] = p
+        d_val[here, :] = jnp.dot(
+            p.astype(BF), three[:, PAIR : PAIR + HEAD], preferred_element_type=F32
+        ).astype(BF)
+
+    def value_rows(t, target):
+        here = pl.ds(pl.multiple_of(t * n, n), n)
+        back = jnp.dot(hot_t[here, :], d_val[...], preferred_element_type=F32).astype(BF)
+        place = pl.ds(pl.multiple_of(t * half, half), half)
+        target[place, :HEAD] = back[:half]
+        target[place, HEAD:] = back[half:]
+
+    for t in peers:
+        value_rows(t, send_dv)
+        remote(block(send_dv, t, half), block(got_dv, me, half), DV + t, DV + me, (dp, t)).start()
+    value_rows(me, got_dv)
+
+    arrived(got_v, V, half)
+    for t in range(HEADS):
+        packed = got_v[t * half : (t + 1) * half, :]
+        tile_v[t * n : t * n + half, :] = packed[:, :HEAD]
+        tile_v[t * n + half : (t + 1) * n, :] = packed[:, HEAD:]
 
     @pl.loop(0, HEADS)
     def _(k):
         here = pl.ds(pl.multiple_of(k * n, n), n)
-        both = jnp.dot(hot[here, :], got_vu[...], preferred_element_type=F32).astype(BF)
-        values, outer = both[:, :HEAD], both[:, HEAD:]
+        values = jnp.dot(hot[here, :], tile_v[...], preferred_element_type=F32).astype(BF)
+        three = win_qku[here, :]
         p = probs[here, :]
-        d_values = jnp.dot(p.astype(BF), outer, preferred_element_type=F32).astype(BF)
-        gp = lax.dot_general(values, outer, NT, preferred_element_type=F32)
+        gp = lax.dot_general(
+            values, three[:, PAIR : PAIR + HEAD], NT, preferred_element_type=F32
+        )
         delta = jnp.sum(p * gp, axis=0, keepdims=True)
         gs = (p * (gp - delta) * scale).astype(BF)
-        queries, keys = win_qk[here, :HEAD], win_qk[here, HEAD:]
+        queries, keys = three[:, :HEAD], three[:, HEAD:PAIR]
         d_win[here, :HEAD] = lax.dot_general(gs, keys, TN, preferred_element_type=F32).astype(BF)
-        d_win[here, HEAD:PAIR] = jnp.dot(gs, queries, preferred_element_type=F32).astype(BF)
-        d_win[here, PAIR : PAIR + HEAD] = d_values
-        d_win[here, PAIR + HEAD :] = jnp.zeros((n, HEAD), BF)
-
-    def to_tile(t, dqk_ref, dv_ref, slot):
+        d_win[here, HEAD:] = jnp.dot(gs, queries, preferred_element_type=F32).astype(BF)
+
+    def to_tile(t, target):
         here = pl.ds(pl.multiple_of(t * n, n), n)
-        back = jnp.dot(hot_t[here, :], d_win[...], preferred_element_type=F32).astype(BF)
-        dqk_ref[pl.ds(pl.multiple_of(slot * n, n), n), :] = back[:, :PAIR]
-        place = pl.ds(pl.multiple_of(slot * half, half), half)
-        dv_ref[place, :HEAD] = back[:half, PAIR : PAIR + HEAD]
-        dv_ref[place, HEAD:] = back[half:, PAIR : PAIR + HEAD]
-
-    for t in peers:
-        to_tile(t, send_dqk, send_dv, t)
+        target[here, :] = jnp.dot(
+            hot_t[here, :], d_win[...], preferred_element_type=F32
+        ).astype(BF)
+
+    for t in peers:
+        to_tile(t, send_dqk)
         remote(block(send_dqk, t, n), block(got_dqk, me, n), DQK + t, DQK + me, (dp, t)).start()
-        remote(block(send_dv, t, half), block(got_dv, me, half), DV + t, DV + me, (dp, t)).start()
-    to_tile(me, got_dqk, got_dv, me)
+    to_tile(me, got_dqk)
+    arrived(got_dv, DV, half)
     arrived(got_dqk, DQK, n)
-    arrived(got_dv, DV, half)
     for h in range(HEADS):
         rows[:, h * HEAD : (h + 1) * HEAD] = got_dqk[h * n : (h + 1) * n, :HEAD]
         rows[:, inner + h * HEAD : inner + (h + 1) * HEAD] = got_dqk[h * n : (h + 1) * n, HEAD:]
@@ -427,15 +463,16 @@
     remote(total.at[other1], total.at[other1], G1, G1, (peer_1, me)).wait_recv()
     back0 = remote(total.at[at(off0, d1)], total.at[at(off0, d1)], G0, G0, (peer_c, me))
     back0.start()
-    gw_out[at(off0, d1), :] = total[at(off0, d1), :].astype(F32)
+    gw_out[at(off0, d1), :] = total[at(off0, d1), :]
     back0.wait_send()
     remote(total.at[other0], total.at[other0], G0, G0, (peer_c, me)).wait_recv()
-    gw_out[other0, :] = total[other0, :].astype(F32)
+    gw_out[other0, :] = total[other0, :]
 
     for t in peers:
         remote(pos, pos, POS + t, POS + t, (dp, t)).wait_send()
         remote(block(send_qk, t, n), block(send_qk, t, n), QK + t, QK + t, (dp, t)).wait_send()
-        remote(block(send_vu, t, n), block(send_vu, t, n), VU + t, VU + t, (dp, t)).wait_send()
+        remote(block(send_u, t, half), block(send_u, t, half), U + t, U + t, (dp, t)).wait_send()
+        remote(block(send_v, t, half), block(send_v, t, half), V + t, V + t, (dp, t)).wait_send()
         remote(block(send_dqk, t, n), block(send_dqk, t, n), DQK + t, DQK + t, (dp, t)).wait_send()
         remote(block(send_dv, t, half), block(send_dv, t, half), DV + t, DV + t, (dp, t)).wait_send()
         piece = stage.at[at(off2 + t * d4, d4)]
@@ -454,7 +491,7 @@
         fused,
         out_shape=(
             jax.ShapeDtypeStruct((n, width), BF),
-            jax.ShapeDtypeStruct((width, cols), F32),
+            jax.ShapeDtypeStruct((width, cols), BF),
             jax.ShapeDtypeStruct((8, width), F32),
         ),
         in_specs=[vmem] * 6,
@@ -465,14 +502,19 @@
             pltpu.VMEM((n, 1), F32),
             pltpu.VMEM((HEADS, 8, n), jnp.int32),
             pltpu.VMEM((all_rows, PAIR), BF),
+            pltpu.VMEM((all_rows // 2, PAIR), BF),
+            pltpu.VMEM((all_rows // 2, PAIR), BF),
             pltpu.VMEM((all_rows, PAIR), BF),
-            pltpu.VMEM((all_rows, PAIR), BF),
-            pltpu.VMEM((all_rows, PAIR), BF),
+            pltpu.VMEM((all_rows // 2, PAIR), BF),
+            pltpu.VMEM((all_rows // 2, PAIR), BF),
+            pltpu.VMEM((all_rows, 2 * PAIR), BF),
+            pltpu.VMEM((all_rows, HEAD), BF),
             pltpu.VMEM((all_rows, all_rows), BF),
             pltpu.VMEM((all_rows, all_rows), BF),
+            pltpu.VMEM((all_rows, 2 * PAIR), BF),
+            pltpu.VMEM((all_rows, n), F32),
+            pltpu.VMEM((all_rows, HEAD), BF),
             pltpu.VMEM((all_rows, PAIR), BF),
-            pltpu.VMEM((all_rows, n), F32),
-            pltpu.VMEM((all_rows, 2 * PAIR), BF),
             pltpu.VMEM((all_rows, PAIR), BF),
             pltpu.VMEM((all_rows // 2, PAIR), BF),
             pltpu.VMEM((all_rows, PAIR), BF),
@@ -495,7 +537,7 @@
             collective_id=0, has_side_effects=True, vmem_limit_bytes=56 * 2**20
         ),
     )(features[0], upstream_grad[0], pos, gain[None], bias[None], w_qkv)
-    return grad_in[None], grad_w, small[0], small[1]
+    return grad_in[None], grad_w.astype(F32), small[0], small[1]
 
 
 def solution(mesh):

time: 100 us -> 99.1 us (level)
  local copies, waits for them, and re-layouts: 6.51 us -> 2.79 us
  other arithmetic: 0.7 us -> 3.09 us
    unnamed x2 -> x3, local copies, waits for them, and re-layouts: 4.52 us -> 0.8 us
    convert_element_type x0 -> x1, other arithmetic: none -> 2.38 us  [by_heads(): return (grad_in[None], grad_w.astype(F32), small[0], small[1])]
where the time goes in v2:
time: 99.1 us; the launch traced here: 98.9 us
  Pallas kernels  92.3 us (93%)
  other arithmetic  3.09 us (3%)
  local copies, waits for them, and re-layouts  2.79 us (3%)
    pallas_call x1, Pallas kernels, by_heads(): pl.pallas_call(fused, out_shape=(jax.ShapeDtypeStruct((n, width), BF), ja...  92.3 us
    convert_element_type x1, other arithmetic, by_heads(): return (grad_in[None], grad_w.astype(F32), small[0], small[1])  2.38 us

profile of v2, /device:TPU:0, one launch (start us, length us, event | category | flops | bytes accessed | tf_op | source)
XLA Modules:
  0.0 98.9 jit_solution(13990555819289176881)
XLA Ops:
  0.6 0.7 multiply_add_fusion
  1.3 0.6 broadcast_in_dim.17.pos
  1.9 92.3 %shard_map.102 = (bf16[512,512]{1,0:T(8,128)(2,1)}, bf16[512,768]{1,0:T(8,128)(2,1)}, f32[8,512]{1,0:T(8,128)}) custom-call(bf16[512,512]{1,0:T(8,128)(2,1)} %bitcast.8, bf16[512,256]{1,0:T(8,128)(2,1)} %bitcast.10, s32[8,512]{1,0:T(8,128)} %broadcast_in_dim.17.pos, f32[1,512]{1,0:T(1,128)} %bitcast.12, f32[1,512]{1,0:T(1,128)} %bitcast.13, bf16[512,768]{1,0:T(8,128)(2,1)} %w.1), custom_call_target="tpu_custom_call" | custom-call | tf_op jit(solution)/shard_map/pallas_call | solution.py:490
  94.3 0.0 copy-start
  94.3 1.4 %fusion = (f32[1,512]{1,0:T(1,128)}, f32[1,512]{1,0:T(1,128)}) fusion(f32[8,512]{1,0:T(8,128)} %get-tuple-element.9), kind=kLoop, calls=%fused_computation.1 | loop fusion | bytes 8192 | tf_op jit(solution)/shard_map/slice | solution.py:540
  95.7 2.4 %convert_element_type.3 = f32[512,768]{1,0:T(8,128)} convert(bf16[512,768]{1,0:T(8,128)(2,1)} %get-tuple-element.8) | non-fusion elementwise | flops 393216 | bytes 2359296 | tf_op jit(solution)/shard_map/convert_element_type | solution.py:540
  98.1 0.0 copy-done
  98.1 0.8 copy.12
Async XLA Ops:
  94.3 3.8 %copy-start = (bf16[512,512]{1,0:T(8,128)(2,1)S(1)}, bf16[512,512]{1,0:T(8,128)(2,1)}, u32[]{:S(2)}) copy-start(bf16[512,512]{1,0:T(8,128)(2,1)} %get-tuple-element.7) | copy-start | bytes 1572868

commit v3 on v2

--- a/solution.py
+++ b/solution.py
@@ -142,9 +142,11 @@
 NT = (((1,), (1,)), ((), ()))
 TN = (((0,), (0,)), ((), ()))
 
-POS, QK, U, V, DQK, DV, RZ, GZ, SZ = (4 * i for i in range(9))
-R0, R1, R2, G0, G1, G2, S0, S1, S2 = range(36, 45)
-N_SEM = 45
+POS, QK, U, V, DQK, DV, SZ = (4 * i for i in range(7))
+S0, S1, S2 = 28, 29, 30
+R0, R1, R2, G0, G1, G2 = (31 + 3 * i for i in range(6))
+RZ, GZ = 49, 61
+N_SEM = 73
 
 
 def fused(
@@ -352,19 +354,7 @@
         to_tile(t, send_dqk)
         remote(block(send_dqk, t, n), block(got_dqk, me, n), DQK + t, DQK + me, (dp, t)).start()
     to_tile(me, got_dqk)
-    arrived(got_dv, DV, half)
-    arrived(got_dqk, DQK, n)
-    for h in range(HEADS):
-        rows[:, h * HEAD : (h + 1) * HEAD] = got_dqk[h * n : (h + 1) * n, :HEAD]
-        rows[:, inner + h * HEAD : inner + (h + 1) * HEAD] = got_dqk[h * n : (h + 1) * n, HEAD:]
-        v_at = 2 * inner + h * HEAD
-        rows[:half, v_at : v_at + HEAD] = got_dv[h * half : (h + 1) * half, :HEAD]
-        rows[half:, v_at : v_at + HEAD] = got_dv[h * half : (h + 1) * half, HEAD:]
-
-    g = lax.dot_general(normed[...], rows[...], TN, preferred_element_type=F32)
-    acc[...] = g
-    stage[...] = g.astype(BF)
-    depth = acc.shape[0]
+    depth = acc.shape[1]
     d1, d2, d3, d4 = depth // 2, depth // 4, depth // 8, depth // 32
     b1 = (1 - c) * bx + c * by
     b2 = (1 - c) * by + c * bx
@@ -374,99 +364,162 @@
     off1 = off0 + b1 * d2
     off2 = off1 + b2 * d3
     off3 = off2 + me * d4
+    windows = lax.axis_size("dp") * lax.axis_size("win")
 
     def at(off, size):
         return pl.ds(pl.multiple_of(off, size), size)
 
+    keep0, keep1, keep2, mine = at(off0, d1), at(off1, d2), at(off2, d3), at(off3, d4)
     other0 = at((1 - c) * d1, d1)
     other1 = at(off0 + (1 - b1) * d2, d2)
     other2 = at(off1 + (1 - b2) * d3, d3)
 
-    step0 = remote(stage.at[other0], rb0, R0, R0, (peer_c, me))
-    step0.start()
+    def halving0(j):
+        return remote(stage.at[j, other0], rb0.at[j], R0 + j, R0 + j, (peer_c, me))
+
+    def halving1(j):
+        return remote(stage.at[j, other1], rb1.at[j], R1 + j, R1 + j, (peer_1, me))
+
+    def halving2(j):
+        return remote(stage.at[j, other2], rb2.at[j], R2 + j, R2 + j, (peer_2, me))
+
+    def reduce0(j):
+        g = lax.dot_general(
+            normed[...], rows[:, j * inner : (j + 1) * inner], TN, preferred_element_type=F32
+        )
+        acc[j] = g
+        stage[j] = g.astype(BF)
+        halving0(j).start()
+
+    def reduce1(j):
+        halving0(j).wait()
+        g = acc[j, keep0, :] + rb0[j].astype(F32)
+        acc[j, keep0, :] = g
+        stage[j, keep0, :] = g.astype(BF)
+        halving1(j).start()
+
+    def reduce2(j):
+        halving1(j).wait()
+        g = acc[j, keep1, :] + rb1[j].astype(F32)
+        acc[j, keep1, :] = g
+        stage[j, keep1, :] = g.astype(BF)
+        halving2(j).start()
+
+    def piece(j, t):
+        return stage.at[j, at(off2 + t * d4, d4)]
+
+    def reduce_z(j):
+        halving2(j).wait()
+        g = acc[j, keep2, :] + rb2[j].astype(F32)
+        acc[j, keep2, :] = g
+        stage[j, keep2, :] = g.astype(BF)
+        for t in peers:
+            remote(piece(j, t), rbz.at[j, me], RZ + 4 * j + t, RZ + 4 * j + me, (dp, t)).start()
+
+    def gather_z(j):
+        own = acc[j, mine, :]
+        for t in peers:
+            got = rbz.at[j, t]
+            remote(got, got, RZ + 4 * j + t, RZ + 4 * j + t, (dp, t)).wait_recv()
+            own += rbz[j, t].astype(F32)
+        total[j, mine, :] = (own * (1.0 / windows)).astype(BF)
+        done = total.at[j, mine]
+        for t in peers:
+            remote(done, done, GZ + 4 * j + t, GZ + 4 * j + me, (dp, t)).start()
+
+    def doubling(j, block_, sem, peer):
+        return remote(total.at[j, block_], total.at[j, block_], sem + j, sem + j, (peer, me))
+
+    def gather2(j):
+        for t in peers:
+            there = total.at[j, at(off2 + t * d4, d4)]
+            remote(there, there, GZ + 4 * j + t, GZ + 4 * j + t, (dp, t)).wait_recv()
+        doubling(j, keep2, G2, peer_2).start()
+
+    def gather1(j):
+        doubling(j, keep2, G2, peer_2).wait_send()
+        doubling(j, other2, G2, peer_2).wait_recv()
+        doubling(j, keep1, G1, peer_1).start()
+
+    def gather0(j):
+        doubling(j, keep1, G1, peer_1).wait_send()
+        doubling(j, other1, G1, peer_1).wait_recv()
+        doubling(j, keep0, G0, peer_c).start()
+
+    def finish_gather(j):
+        doubling(j, keep0, G0, peer_c).wait_send()
+        doubling(j, other0, G0, peer_c).wait_recv()
+        gw_out[:, j * inner : (j + 1) * inner] = total[j]
+
+    arrived(got_dv, DV, half)
+    for h in range(HEADS):
+        v_at = 2 * inner + h * HEAD
+        rows[:half, v_at : v_at + HEAD] = got_dv[h * half : (h + 1) * half, :HEAD]
+        rows[half:, v_at : v_at + HEAD] = got_dv[h * half : (h + 1) * half, HEAD:]
+    reduce0(2)
+    reduce1(2)
+    reduce2(2)
+    reduce_z(2)
+
+    arrived(got_dqk, DQK, n)
+    for h in range(HEADS):
+        rows[:, h * HEAD : (h + 1) * HEAD] = got_dqk[h * n : (h + 1) * n, :HEAD]
+        rows[:, inner + h * HEAD : inner + (h + 1) * HEAD] = got_dqk[h * n : (h + 1) * n, HEAD:]
+    reduce0(0)
+    reduce0(1)
+    reduce1(0)
+    reduce1(1)
 
     gn = lax.dot_general(rows[...], w[...], NT, preferred_element_type=F32)
     u = unit[...]
     row_id = lax.broadcasted_iota(jnp.int32, (8, gn.shape[1]), 0)
-    small = jnp.where(
+    small_send[0] = jnp.where(
         row_id == 0,
         jnp.sum(gn * u, axis=0, keepdims=True),
         jnp.where(row_id == 1, jnp.sum(gn, axis=0, keepdims=True), 0.0),
     )
-    small_send[0] = small
     small0 = remote(small_send.at[0], small_got.at[0], S0, S0, (peer_c, me))
     small0.start()
+    reduce2(0)
+    reduce2(1)
+    gather_z(2)
     gh = gn * gain[...]
     first = jnp.mean(gh, axis=1, keepdims=True)
     second = jnp.mean(gh * u, axis=1, keepdims=True)
     grad_in[...] = (inv[...] * (gh - first - u * second)).astype(BF)
 
-    step0.wait()
-    keep = at(off0, d1)
-    acc[keep, :] += rb0[...].astype(F32)
-    stage[keep, :] = acc[keep, :].astype(BF)
-    step1 = remote(stage.at[other1], rb1, R1, R1, (peer_1, me))
-    step1.start()
     small0.wait()
     small_send[1] = small_send[0] + small_got[0]
     small1 = remote(small_send.at[1], small_got.at[1], S1, S1, (peer_x, me))
     small1.start()
-
-    step1.wait()
-    keep = at(off1, d2)
-    acc[keep, :] += rb1[...].astype(F32)
-    stage[keep, :] = acc[keep, :].astype(BF)
-    step2 = remote(stage.at[other2], rb2, R2, R2, (peer_2, me))
-    step2.start()
+    reduce_z(0)
+    reduce_z(1)
+    gather2(2)
     small1.wait()
     small_send[2] = small_send[1] + small_got[1]
     small2 = remote(small_send.at[2], small_got.at[2], S2, S2, (peer_y, me))
     small2.start()
-
-    step2.wait()
-    keep = at(off2, d3)
-    acc[keep, :] += rb2[...].astype(F32)
-    stage[keep, :] = acc[keep, :].astype(BF)
-    for t in peers:
-        remote(stage.at[at(off2 + t * d4, d4)], rbz.at[me], RZ + t, RZ + me, (dp, t)).start()
+    gather_z(0)
+    gather_z(1)
+    gather1(2)
     small2.wait()
     small_send[3] = small_send[2] + small_got[2]
     for t in peers:
         remote(small_send.at[3], small_z.at[me], SZ + t, SZ + me, (dp, t)).start()
     small_z[me] = small_send[3]
-
-    mine = at(off3, d4)
-    for t in peers:
-        remote(rbz.at[t], rbz.at[t], RZ + t, RZ + t, (dp, t)).wait_recv()
-    own = acc[mine, :]
-    for t in peers:
-        own += rbz[t].astype(F32)
-    windows = lax.axis_size("dp") * lax.axis_size("win")
-    total[mine, :] = (own * (1.0 / windows)).astype(BF)
-
-    for t in peers:
-        remote(total.at[mine], total.at[mine], GZ + t, GZ + me, (dp, t)).start()
-    for t in peers:
-        there = total.at[at(off2 + t * d4, d4)]
-        remote(there, there, GZ + t, GZ + t, (dp, t)).wait_recv()
-    back2 = remote(total.at[at(off2, d3)], total.at[at(off2, d3)], G2, G2, (peer_2, me))
-    back2.start()
+    gather2(0)
+    gather2(1)
+    gather0(2)
+    gather1(0)
+    gather1(1)
+    finish_gather(2)
+    gather0(0)
+    gather0(1)
     for t in peers:
         remote(small_z.at[t], small_z.at[t], SZ + t, SZ + t, (dp, t)).wait_recv()
     gs_out[...] = (small_z[0] + small_z[1] + small_z[2] + small_z[3]) * (1.0 / windows)
-
-    back2.wait_send()
-    remote(total.at[other2], total.at[other2], G2, G2, (peer_2, me)).wait_recv()
-    back1 = remote(total.at[at(off1, d2)], total.at[at(off1, d2)], G1, G1, (peer_1, me))
-    back1.start()
-    back1.wait_send()
-    remote(total.at[other1], total.at[other1], G1, G1, (peer_1, me)).wait_recv()
-    back0 = remote(total.at[at(off0, d1)], total.at[at(off0, d1)], G0, G0, (peer_c, me))
-    back0.start()
-    gw_out[at(off0, d1), :] = total[at(off0, d1), :]
-    back0.wait_send()
-    remote(total.at[other0], total.at[other0], G0, G0, (peer_c, me)).wait_recv()
-    gw_out[other0, :] = total[other0, :]
+    finish_gather(0)
+    finish_gather(1)
 
     for t in peers:
         remote(pos, pos, POS + t, POS + t, (dp, t)).wait_send()
@@ -475,9 +528,10 @@
         remote(block(send_v, t, half), block(send_v, t, half), V + t, V + t, (dp, t)).wait_send()
         remote(block(send_dqk, t, n), block(send_dqk, t, n), DQK + t, DQK + t, (dp, t)).wait_send()
         remote(block(send_dv, t, half), block(send_dv, t, half), DV + t, DV + t, (dp, t)).wait_send()
-        piece = stage.at[at(off2 + t * d4, d4)]
-        remote(piece, piece, RZ + t, RZ + t, (dp, t)).wait_send()
-        remote(total.at[mine], total.at[mine], GZ + t, GZ + t, (dp, t)).wait_send()
+        for j in range(3):
+            done = total.at[j, mine]
+            remote(piece(j, t), piece(j, t), RZ + 4 * j + t, RZ + 4 * j + t, (dp, t)).wait_send()
+            remote(done, done, GZ + 4 * j + t, GZ + 4 * j + t, (dp, t)).wait_send()
         remote(small_send.at[3], small_send.at[3], SZ + t, SZ + t, (dp, t)).wait_send()
 
 
@@ -520,13 +574,13 @@
             pltpu.VMEM((all_rows, PAIR), BF),
             pltpu.VMEM((all_rows // 2, PAIR), BF),
             pltpu.VMEM((n, cols), BF),
-            pltpu.VMEM((width, cols), F32),
-            pltpu.VMEM((width, cols), BF),
-            pltpu.VMEM((width // 2, cols), BF),
-            pltpu.VMEM((width // 4, cols), BF),
-            pltpu.VMEM((width // 8, cols), BF),
-            pltpu.VMEM((HEADS, width // 32, cols), BF),
-            pltpu.VMEM((width, cols), BF),
+            pltpu.VMEM((3, width, cols // 3), F32),
+            pltpu.VMEM((3, width, cols // 3), BF),
+            pltpu.VMEM((3, width // 2, cols // 3), BF),
+            pltpu.VMEM((3, width // 4, cols // 3), BF),
+            pltpu.VMEM((3, width // 8, cols // 3), BF),
+            pltpu.VMEM((3, HEADS, width // 32, cols // 3), BF),
+            pltpu.VMEM((3, width, cols // 3), BF),
             pltpu.VMEM((4, 8, width), F32),
             pltpu.VMEM((3, 8, width), F32),
             pltpu.VMEM((HEADS, 8, width), F32),

time: 99.1 us -> 96 us (0.969)
  Pallas kernels: 92.3 us -> 89.1 us
    pallas_call x1, Pallas kernels: 92.3 us -> 89.1 us  [by_heads(): pl.pallas_call(fused, out_shape=(jax.ShapeDtypeStruct((n, width), BF), ja...]
where the time goes in v3:
time: 96 us; the launch traced here: 95.7 us
  Pallas kernels  89.1 us (93%)
  other arithmetic  3.09 us (3%)
  local copies, waits for them, and re-layouts  2.79 us (3%)
    pallas_call x1, Pallas kernels, by_heads(): pl.pallas_call(fused, out_shape=(jax.ShapeDtypeStruct((n, width), BF), ja...  89.1 us
    convert_element_type x1, other arithmetic, by_heads(): return (grad_in[None], grad_w.astype(F32), small[0], small[1])  2.38 us

profile of v3, /device:TPU:0, one launch (start us, length us, event | category | flops | bytes accessed | tf_op | source)
XLA Modules:
  0.0 95.7 jit_solution(297327717273831305)
XLA Ops:
  0.6 0.7 multiply_add_fusion
  1.3 0.6 broadcast_in_dim.17.pos
  1.9 89.1 %shard_map.102 = (bf16[512,512]{1,0:T(8,128)(2,1)}, bf16[512,768]{1,0:T(8,128)(2,1)}, f32[8,512]{1,0:T(8,128)}) custom-call(bf16[512,512]{1,0:T(8,128)(2,1)} %bitcast.8, bf16[512,256]{1,0:T(8,128)(2,1)} %bitcast.10, s32[8,512]{1,0:T(8,128)} %broadcast_in_dim.17.pos, f32[1,512]{1,0:T(1,128)} %bitcast.12, f32[1,512]{1,0:T(1,128)} %bitcast.13, bf16[512,768]{1,0:T(8,128)(2,1)} %w.1), custom_call_target="tpu_custom_call" | custom-call | tf_op jit(solution)/shard_map/pallas_call | solution.py:544
  91.1 0.0 copy-start
  91.1 1.4 %fusion = (f32[1,512]{1,0:T(1,128)}, f32[1,512]{1,0:T(1,128)}) fusion(f32[8,512]{1,0:T(8,128)} %get-tuple-element.9), kind=kLoop, calls=%fused_computation.1 | loop fusion | bytes 8192 | tf_op jit(solution)/shard_map/slice | solution.py:594
  92.5 2.4 %convert_element_type.3 = f32[512,768]{1,0:T(8,128)} convert(bf16[512,768]{1,0:T(8,128)(2,1)} %get-tuple-element.8) | non-fusion elementwise | flops 393216 | bytes 2359296 | tf_op jit(solution)/shard_map/convert_element_type | solution.py:594
  94.9 0.0 copy-done
  94.9 0.8 copy.12
Async XLA Ops:
  91.1 3.8 %copy-start = (bf16[512,512]{1,0:T(8,128)(2,1)S(1)}, bf16[512,512]{1,0:T(8,128)(2,1)}, u32[]{:S(2)}) copy-start(bf16[512,512]{1,0:T(8,128)(2,1)} %get-tuple-element.7) | copy-start | bytes 1572868

commit v4 on v3

--- a/solution.py
+++ b/solution.py
@@ -152,7 +152,8 @@
 def fused(
     feat,
     up,
-    pos,
+    window,
+    slot,
     gain,
     bias,
     w,
@@ -236,9 +237,9 @@
         for t in peers:
             remote(block(target, t, size), block(target, t, size), base + t, base + t, (dp, t)).wait_recv()
 
+    pos_all[me] = jnp.broadcast_to(window[...] * n + slot[...], (8, n))
     for t in peers:
-        remote(pos, pos_all.at[me], POS + t, POS + me, (dp, t)).start()
-    pos_all[me] = pos[...]
+        remote(pos_all.at[me], pos_all.at[me], POS + t, POS + me, (dp, t)).start()
 
     for h in range(HEADS):
         send_u[h * half : (h + 1) * half, :HEAD] = up[:half, h * HEAD : (h + 1) * HEAD]
@@ -522,7 +523,7 @@
     finish_gather(1)
 
     for t in peers:
-        remote(pos, pos, POS + t, POS + t, (dp, t)).wait_send()
+        remote(pos_all.at[me], pos_all.at[me], POS + t, POS + t, (dp, t)).wait_send()
         remote(block(send_qk, t, n), block(send_qk, t, n), QK + t, QK + t, (dp, t)).wait_send()
         remote(block(send_u, t, half), block(send_u, t, half), U + t, U + t, (dp, t)).wait_send()
         remote(block(send_v, t, half), block(send_v, t, half), V + t, V + t, (dp, t)).wait_send()
@@ -539,7 +540,6 @@
     n, width = features.shape[1:]
     cols = w_qkv.shape[1]
     all_rows = HEADS * n
-    pos = jnp.broadcast_to(window_of * n + window_slot, (8, n))
     vmem = pl.BlockSpec(memory_space=pltpu.VMEM)
     grad_in, grad_w, small = pl.pallas_call(
         fused,
@@ -548,7 +548,7 @@
             jax.ShapeDtypeStruct((width, cols), BF),
             jax.ShapeDtypeStruct((8, width), F32),
         ),
-        in_specs=[vmem] * 6,
+        in_specs=[vmem] * 7,
         out_specs=(vmem, vmem, vmem),
         scratch_shapes=[
             pltpu.VMEM((n, width), F32),
@@ -590,7 +590,7 @@
         compiler_params=pltpu.CompilerParams(
             collective_id=0, has_side_effects=True, vmem_limit_bytes=56 * 2**20
         ),
-    )(features[0], upstream_grad[0], pos, gain[None], bias[None], w_qkv)
+    )(features[0], upstream_grad[0], window_of, window_slot, gain[None], bias[None], w_qkv)
     return grad_in[None], grad_w.astype(F32), small[0], small[1]
 
 

time: 96 us -> 94.6 us (0.985)
  no operation moved by 1% of the time
where the time goes in v4:
time: 94.6 us; the launch traced here: 94.4 us
  Pallas kernels  89.2 us (94%)
  other arithmetic  2.38 us (3%)
  local copies, waits for them, and re-layouts  2.18 us (2%)
    pallas_call x1, Pallas kernels, by_heads(): pl.pallas_call(fused, out_shape=(jax.ShapeDtypeStruct((n, width), BF), ja...  89.2 us
    convert_element_type x1, other arithmetic, by_heads(): return (grad_in[None], grad_w.astype(F32), small[0], small[1])  2.38 us

profile of v4, /device:TPU:0, one launch (start us, length us, event | category | flops | bytes accessed | tf_op | source)
XLA Modules:
  0.0 94.4 jit_solution(14764525743162773664)
XLA Ops:
  0.6 89.2 %shard_map.102 = (bf16[512,512]{1,0:T(8,128)(2,1)}, bf16[512,768]{1,0:T(8,128)(2,1)}, f32[8,512]{1,0:T(8,128)}) custom-call(bf16[512,512]{1,0:T(8,128)(2,1)} %bitcast.7, bf16[512,256]{1,0:T(8,128)(2,1)} %bitcast.9, s32[1,512]{1,0:T(1,128)} %window.1, s32[1,512]{1,0:T(1,128)} %slot.1, f32[1,512]{1,0:T(1,128)} %bitcast.10, f32[1,512]{1,0:T(1,128)} %bitcast.11, ...), custom_call_target="tpu_custom_call" | custom-call | tf_op jit(solution)/shard_map/pallas_call | solution.py:544
  89.8 0.0 copy-start
  89.8 1.4 %fusion = (f32[1,512]{1,0:T(1,128)}, f32[1,512]{1,0:T(1,128)}) fusion(f32[8,512]{1,0:T(8,128)} %get-tuple-element.9), kind=kLoop, calls=%fused_computation | loop fusion | bytes 8192 | tf_op jit(solution)/shard_map/slice | solution.py:594
  91.2 2.4 %convert_element_type.3 = f32[512,768]{1,0:T(8,128)} convert(bf16[512,768]{1,0:T(8,128)(2,1)} %get-tuple-element.8) | non-fusion elementwise | flops 393216 | bytes 2359296 | tf_op jit(solution)/shard_map/convert_element_type | solution.py:594
  93.6 0.0 copy-done
  93.6 0.8 copy.12
Async XLA Ops:
  89.8 3.8 %copy-start = (bf16[512,512]{1,0:T(8,128)(2,1)S(1)}, bf16[512,512]{1,0:T(8,128)(2,1)}, u32[]{:S(2)}) copy-start(bf16[512,512]{1,0:T(8,128)(2,1)} %get-tuple-element.7) | copy-start | bytes 1572868
